TPU v7x, 32 devices: a whole 2x2x4 slice. The times are simulated.
32 devices in a mesh: batch: 4 (over y, x), ctx: 8 (over z, core).
Axes of the slice: x: 2, y: 2, z: 4, core: 2. Of those that a mesh axis runs over, the one named last changes fastest.
Arguments:
- inner_x: bfloat16 [4, 512, 8192], P('batch', 'ctx'), may hold values from -6 to 6
- inner_bc: bfloat16 [4, 512, 1024], P('batch', 'ctx'), may hold values from -6 to 6
- step_size: float32 [4, 512, 64], P('batch', 'ctx'), may hold values from 0.1 to 1400, as said below
- decay_base: float32 [64], replicated, may hold values from 0.9995 to 0.9998
- conv_inner: float32 [4, 8192], replicated, may hold values from -3 to 3
- conv_groups: float32 [4, 1024], replicated, may hold values from -3 to 3
- norm_gain: float32 [8192], replicated, may hold values from 0.5 to 1.5
- cache_pool: bfloat16 [16, 64, 128, 128], P('batch', 'ctx'), may hold values from -0.59765625 to 0.59765625
- reuse_owner: int32 [4], replicated, may hold values from 0 to 3
- reuse_level: int32 [4], replicated, may hold values from 0 to 4, as said below
- prompt_blocks: int32 [4], replicated, may hold values from 1 to 2
Outputs:
- mixer_out: bfloat16 [4, 512, 8192], P('batch', 'ctx')
Inputs may be any that keep to these rules, and one draw needn't show every extreme that they name: `step_size`: positive step sizes. `reuse_level`: 0 means nothing is cached; level l names the owner's l-th cached state.
All inputs are finite; a program needn't handle non-finite values.
Results may differ from a plain program's by a relative error of at most 0.009.
Values may be sent and summed in bfloat16 or wider, within the bound.
A program may use at most 64 MiB of HBM per device.

v0:
```python
import jax
import jax.numpy as jnp
from jax import lax
from jax.sharding import PartitionSpec as P

LOCAL_HEADS = 64
P_SIZE = 128
N = 128
GROUPS = 4
KCONV = 4
LEN_BLOCK = 256


def shifted(value, axis, steps):
    count = lax.axis_size(axis)
    first, last = (max(0, -steps), min(count, count - steps))
    return lax.ppermute(value, axis, [(source, source + steps) for source in range(first, last)])


def convolve(extended, weight, length):
    summed = jnp.zeros((length, extended.shape[1]), jnp.float32)
    for offset in range(weight.shape[0]):
        summed = summed + weight[offset] * extended[offset : offset + length].astype(jnp.float32)
    return jax.nn.silu(summed).astype(jnp.bfloat16)


def block_local(conv_x, write_proj, read_proj, log_step):
    length = log_step.shape[0]
    per_group = LOCAL_HEADS // GROUPS
    cumul = jnp.cumsum(log_step, axis=0)
    inject = -jnp.expm1(log_step)
    inner_heads = conv_x.reshape(length, GROUPS, per_group, P_SIZE)
    write_groups = write_proj.reshape(length, GROUPS, N)
    read_groups = read_proj.reshape(length, GROUPS, N)
    scores = jnp.einsum(
        "tgn,sgn->gts", read_groups, write_groups, preferred_element_type=jnp.float32
    )
    row_index = jnp.arange(length)[:, None]
    col_index = jnp.arange(length)[None, :]
    cumul_heads = cumul.T.reshape(GROUPS, per_group, length)
    inject_heads = inject.T.reshape(GROUPS, per_group, length)
    exponent_gap = cumul_heads[:, :, :, None] - cumul_heads[:, :, None, :]
    exponent_gap = jnp.where(row_index >= col_index, exponent_gap, -jnp.inf)
    mixing = (scores[:, None] * jnp.exp(exponent_gap) * inject_heads[:, :, None, :]).astype(
        jnp.bfloat16
    )
    intra_part = jnp.einsum(
        "gkts,sgkp->tgkp", mixing, inner_heads, preferred_element_type=jnp.float32
    )
    tail_weight = jnp.exp(cumul[-1][None, :] - cumul) * inject
    weighted = (inner_heads * tail_weight.reshape(length, GROUPS, per_group)[..., None]).astype(
        jnp.bfloat16
    )
    end_state = jnp.einsum(
        "sgkp,sgn->gkpn", weighted, write_groups, preferred_element_type=jnp.float32
    )
    end_state = end_state.reshape(LOCAL_HEADS, P_SIZE, N).astype(jnp.bfloat16)
    block_decay = jnp.exp(cumul[-1]).astype(jnp.bfloat16)
    return (intra_part.reshape(length, LOCAL_HEADS, P_SIZE), cumul, end_state, block_decay)


def block_output(intra_part, cumul, read_proj, incoming, norm_gain, live):
    length = cumul.shape[0]
    per_group = LOCAL_HEADS // GROUPS
    read_groups = read_proj.reshape(length, GROUPS, N)
    state_groups = incoming.reshape(GROUPS, per_group, P_SIZE, N)
    inter_part = jnp.einsum(
        "tgn,gkpn->tgkp", read_groups, state_groups, preferred_element_type=jnp.float32
    ).reshape(length, LOCAL_HEADS, P_SIZE)
    summed = intra_part + jnp.exp(cumul)[:, :, None] * inter_part
    inv_scale = lax.rsqrt(jnp.mean(summed * summed, axis=2, keepdims=True) + 1e-05)
    result = summed * inv_scale * norm_gain.reshape(LOCAL_HEADS, P_SIZE)
    result = jnp.where(live[:, None, None], result, 0.0)
    return result.reshape(length, LOCAL_HEADS * P_SIZE).astype(jnp.bfloat16)


def advance(running, pieces):
    decay_block, state_block = pieces
    next_state = decay_block.astype(jnp.float32)[:, None, None] * running + state_block.astype(
        jnp.float32
    )
    return (next_state, running)


def body(
    inner_x,
    inner_bc,
    step_size,
    decay_base,
    conv_inner,
    conv_groups,
    norm_gain,
    cache_pool,
    reuse_owner,
    reuse_level,
    prompt_blocks,
):
    length = inner_x.shape[1]
    width_x = inner_x.shape[2]
    request = lax.axis_index("batch")
    ctx_place = lax.axis_index("ctx")
    tail_rows = jnp.concatenate(
        [inner_x[0, length - KCONV + 1 :], inner_bc[0, length - KCONV + 1 :]], axis=1
    )
    tail_rows = shifted(tail_rows, "ctx", 1)
    conv_x = convolve(
        jnp.concatenate([tail_rows[:, :width_x], inner_x[0]], axis=0), conv_inner, length
    )
    conv_bc = convolve(
        jnp.concatenate([tail_rows[:, width_x:], inner_bc[0]], axis=0), conv_groups, length
    )
    positions = ctx_place * length + jnp.arange(length)
    live = positions < prompt_blocks[request] * LEN_BLOCK
    log_step = jnp.where(live[:, None], step_size[0], 0.0) * jnp.log(decay_base)[None, :]
    intra_part, cumul, end_state, block_decay = block_local(
        conv_x, conv_bc[:, : GROUPS * N], conv_bc[:, GROUPS * N :], log_step
    )
    cache_owner = reuse_owner[request]
    cached_level = reuse_level[request]
    slots = cache_pool.shape[0]
    pooled = lax.all_gather(cache_pool, "batch", axis=0, tiled=True)
    slot_index = cache_owner * slots + jnp.maximum(cached_level - 1, 0)
    start_state = lax.dynamic_index_in_dim(pooled, slot_index, 0, keepdims=False)
    start_state = jnp.where(cached_level > 0, start_state, jnp.zeros_like(start_state))
    ctx_count = lax.axis_size("ctx")
    head_share = LOCAL_HEADS // ctx_count
    decays_in, states_in = (
        lax.all_to_all(
            block_decay.reshape(ctx_count, head_share),
            "ctx",
            split_axis=0,
            concat_axis=0,
            tiled=True,
        ),
        lax.all_to_all(
            end_state.reshape(ctx_count, head_share, P_SIZE, N),
            "ctx",
            split_axis=0,
            concat_axis=0,
            tiled=True,
        ),
    )
    last_state, incoming_parts = lax.scan(
        advance, start_state.astype(jnp.float32), (decays_in, states_in)
    )
    returned = lax.all_to_all(
        incoming_parts.astype(jnp.bfloat16), "ctx", split_axis=0, concat_axis=0, tiled=True
    )
    incoming = returned.reshape(LOCAL_HEADS, P_SIZE, N)
    result = block_output(intra_part, cumul, conv_bc[:, GROUPS * N :], incoming, norm_gain, live)
    return result.reshape(1, length, LOCAL_HEADS * P_SIZE)


def solution(mesh):
    return jax.shard_map(
        body,
        mesh=mesh,
        in_specs=(
            P("batch", "ctx", None),
            P("batch", "ctx", None),
            P("batch", "ctx", None),
            P(),
            P(),
            P(),
            P(),
            P("batch", "ctx", None, None),
            P(),
            P(),
            P(),
        ),
        out_specs=P("batch", "ctx", None),
        check_vma=False,
    )
```

profile of v0, /device:TPU:0, one launch (start us, length us, event | category | flops | bytes accessed | tf_op | source)
XLA Modules:
  0.0 178.9 jit_solution(856277272822642632)
XLA Ops:
  9.0 2.4 %collective-permute-start = (bf16[3,9216]{1,0:T(4,128)(2,1)S(1)}, bf16[3,9216]{1,0:T(4,128)(2,1)S(1)}, u32[]{:S(2)}, u32[]{:S(2)}) collective-permute-start(bf16[3,9216]{1,0:T(4,128)(2,1)S(1)} %pad_maximum_fusion.2), channel_id=1, source_target_pairs={{0,1},{1,2},{2,3},{3,4},{4,5},{5,6},{6,7},{8,9},{9,10},{10,11},{11... | collective-permute-start | bytes 165896 | tf_op jit(solution)/shard_map/ppermute | solution.py:17
  12.8 1.2 dynamic_slice.21
  15.8 6.2 %all-to-all-start = ((bf16[8,1,8]{2,1,0:T(2,128)(2,1)}), bf16[8,1,8]{2,1,0:T(2,128)(2,1)S(1)}, u32[]{:S(2)}, u32[]{:S(2)}) async-start(bf16[8,1,8]{2,1,0:T(2,128)(2,1)} %convert_element_type.119), calls=%async_computation | async-start | bytes 8192 | tf_op jit(solution)/shard_map/all_to_all | solution.py:128
  22.3 1.3 fusion.32
  23.9 1.6 fusion.16
  26.8 3.4 %convolution_convert_fusion = bf16[4,16,128,128]{3,2,1,0:T(8,128)(2,1)} fusion(f32[64,4,16]{0,2,1:T(8,128)S(1)} %get-tuple-element.54, bf16[64,4,16,128]{3,2,1,0:T(8,128)(2,1)S(1)} %bitcast.84, bf16[64,4,128,1]{2,1,0,3:T(4,128)(2,1)S(1)} %bitcast.90), kind=kOutput, calls=%fused_computation.12 | convolution fusion | flops 136839168 | bytes 3227648 | tf_op jit(solution)/shard_map/sgkp,sgn->gkpn/dot_general | solution.py:54
  30.2 5.2 %all-to-all-start.1 = ((bf16[8,8,128,128]{3,2,1,0:T(8,128)(2,1)}), bf16[8,8,128,128]{3,2,1,0:T(8,128)(2,1)S(1)}, u32[]{:S(2)}, u32[]{:S(2)}) async-start(bf16[8,8,128,128]{3,2,1,0:T(8,128)(2,1)} %bitcast.28), calls=%async_computation.1 | async-start | bytes 4194304 | tf_op jit(solution)/shard_map/all_to_all | solution.py:135
  38.6 26.1 %all-gather.2.cloned.1.call-done = bf16[16,8,128,128]{3,2,1,0:T(8,128)(2,1)} async-done(((bf16[4,8,128,128]{3,2,1,0:T(8,128)(2,1)}), bf16[16,8,128,128]{3,2,1,0:T(8,128)(2,1)}) %all-gather.2.cloned.1.call-update) | async-done | bytes 4194320 | tf_op jit(solution)/shard_map/all_gather | solution.py:121
  64.6 1.0 bitcast_convert_fusion
  65.6 18.9 %all-to-all-done.1 = bf16[8,8,128,128]{3,2,1,0:T(8,128)(2,1)S(1)} async-done(((bf16[8,8,128,128]{3,2,1,0:T(8,128)(2,1)}), bf16[8,8,128,128]{3,2,1,0:T(8,128)(2,1)S(1)}, u32[]{:S(2)}, u32[]{:S(2)}) %all-to-all-start.1) | async-done | bytes 2097184 | tf_op jit(solution)/shard_map/all_to_all | solution.py:135
  84.5 7.4 %while.12 = (s32[]{:T(128)}, f32[8,128,128]{2,1,0:T(8,128)S(1)}, bf16[8,8,128,128]{3,2,1,0:T(8,128)(2,1)}, bf16[8,8]{1,0:T(8,128)(2,1)S(1)}, bf16[8,8,128,128]{3,2,1,0:T(8,128)(2,1)S(1)}, /*index=5*/s32[]{:T(128)}) while((s32[]{:T(128)}, f32[8,128,128]{2,1,0:T(8,128)S(1)}, bf16[8,8,128,128]{3,2,1,0:T(8,128)(2,1)}, bf16[8,8]{1,0:T(8,128)(2,1)S(1)}, ...), condition=%wide.region_2.3_spmd, body=%wide.region_1.2_spmd.sunk | while | flops 393226 | bytes 2359965 | solution.py:143
  91.9 4.4 %all-to-all-start.2 = ((bf16[8,8,128,128]{3,2,1,0:T(8,128)(2,1)}), bf16[8,8,128,128]{3,2,1,0:T(8,128)(2,1)}, u32[]{:S(2)}, u32[]{:S(2)}) async-start(bf16[8,8,128,128]{3,2,1,0:T(8,128)(2,1)} %get-tuple-element.32), calls=%async_computation.2 | async-start | bytes 4194304 | tf_op jit(solution)/shard_map/all_to_all | solution.py:146
  96.4 1.9 %mul.257 = f32[64,64,128]{2,1,0:T(8,128)} broadcast(f32[64,64]{1,0:T(8,128)S(1)} %exp.43), dimensions={0,1} | broadcast | bytes 2113536 | tf_op jit(solution)/shard_map/mul | solution.py:70
  98.3 1.7 mul.258
  100.2 45.1 %all-to-all-done.2 = bf16[8,8,128,128]{3,2,1,0:T(8,128)(2,1)} async-done(((bf16[8,8,128,128]{3,2,1,0:T(8,128)(2,1)}), bf16[8,8,128,128]{3,2,1,0:T(8,128)(2,1)}, u32[]{:S(2)}, u32[]{:S(2)}) %all-to-all-start.2) | async-done | bytes 2097184 | tf_op jit(solution)/shard_map/all_to_all | solution.py:146
  145.3 2.4 %fusion.4 = f32[64,4,16,128]{3,0,2,1:T(8,128)S(1)} fusion(bf16[64,4,128,1]{2,1,0,3:T(4,128)(2,1)S(1)} %bitcast.89, bf16[4,16,128,128]{3,2,1,0:T(8,128)(2,1)} %bitcast.77), kind=kOutput, calls=%fused_computation.13 | convolution fusion | flops 134217728 | bytes 4259840 | tf_op jit(solution)/shard_map/tgn,gkpn->tgkp/dot_general | solution.py:67
  147.8 2.5 %copy.59 = f32[64,4,16,128]{3,2,1,0:T(8,128)} copy(f32[64,4,16,128]{3,0,2,1:T(8,128)S(1)} %fusion.4) | data formatting | bytes 4194304 | tf_op jit(solution)/shard_map/tgn,gkpn->tgkp/transpose | solution.py:67
  150.3 3.0 %multiply_reduce_fusion = (f32[64,4,16]{0,2,1:T(8,128)S(1)}, f32[64,4,16,128]{3,0,2,1:T(8,128)}) fusion(f32[64,4,16,128]{3,0,2,1:T(8,128)S(1)} %fusion.4, f32[64,4,16]{0,2,1:T(8,128)S(1)} %get-tuple-element.53, bf16[64,4,16,128]{3,2,1,0:T(8,128)(2,1)S(1)} %bitcast.85, f32[4,16,64]{2,1,0:T(8,128)S(1)} %bitcast.98, f32[4,16,64]{2,1,0:T(8,128)S(1)} %bitcast.99, ...), kind=kOutput, calls=%fused_computation.8 | convolution fusion | flops 70512640 | bytes 5378048 | tf_op jit(solution)/shard_map/gkts,sgkp->tgkp/dot_general | solution.py:47
  153.4 2.0 %mul.270 = f32[64,64,128]{2,1,0:T(8,128)} broadcast(f32[64,64]{1,0:T(8,128)S(1)} %copy.60), dimensions={0,1} | broadcast | bytes 2113536 | tf_op jit(solution)/shard_map/mul | solution.py:72
  155.4 2.7 %mul.271 = f32[1,64,8192]{2,1,0:T(8,128)} reshape(f32[64,64,128]{2,1,0:T(8,128)} %mul.270) | data formatting | bytes 4194304 | tf_op jit(solution)/shard_map/mul | solution.py:72
  158.1 4.2 %copy.52 = f32[64,4,16,128]{3,2,1,0:T(8,128)} copy(f32[64,4,16,128]{3,0,2,1:T(8,128)} %get-tuple-element.60) | data formatting | bytes 4194304 | tf_op jit(solution)/shard_map/gkts,sgkp->tgkp/transpose | solution.py:47
  162.3 2.8 %reshape.233 = f32[1,64,8192]{2,1,0:T(8,128)} reshape(f32[64,4,16,128]{3,2,1,0:T(8,128)} %copy.52) | data formatting | bytes 4194304 | tf_op jit(solution)/shard_map/reshape | solution.py:59
  165.0 2.8 %reshape.234 = f32[1,64,8192]{2,1,0:T(8,128)} reshape(f32[64,4,16,128]{3,2,1,0:T(8,128)} %copy.59) | data formatting | bytes 4194304 | tf_op jit(solution)/shard_map/reshape | solution.py:69
  167.8 4.3 %select_convert_fusion = bf16[1,64,8192]{2,1,0:T(8,128)(2,1)} fusion(f32[1,64,8192]{2,1,0:T(8,128)} %mul.271, f32[1,64,8192]{2,1,0:T(8,128)} %reshape.233, f32[1,64,8192]{2,1,0:T(8,128)S(1)} %mul.258, f32[1,64,8192]{2,1,0:T(8,128)} %reshape.234, f32[8192]{0:T(1024)S(1)} %copy-done.4, pred[64]{0:T(512)(128)(4,1)S(1)} %add_compare_fusion), kind=kLoop, calls=%fused_computation.7 | loop fusion | flops 3145728 | bytes 9470016 | tf_op jit(solution)/shard_map/convert_element_type | solution.py:74
  (78 shorter events, 15.6 us)
Async XLA Ops:
  6.5 17.4 %copy-start.2 = (bf16[1,64,8192]{2,1,0:T(8,128)(2,1)S(1)}, bf16[1,64,8192]{2,1,0:T(8,128)(2,1)}, u32[]{:S(2)}) copy-start(bf16[1,64,8192]{2,1,0:T(8,128)(2,1)} %param.13) | copy-start | bytes 3145732
  6.5 17.1 %copy-start.3 = (bf16[1,64,1024]{2,1,0:T(8,128)(2,1)S(1)}, bf16[1,64,1024]{2,1,0:T(8,128)(2,1)}, u32[]{:S(2)}) copy-start(bf16[1,64,1024]{2,1,0:T(8,128)(2,1)} %param.14) | copy-start | bytes 393220
  6.5 17.0 %copy-start.5 = (f32[4,1024]{1,0:T(4,128)S(1)}, f32[4,1024]{1,0:T(4,128)}, u32[]{:S(2)}) copy-start(f32[4,1024]{1,0:T(4,128)} %param.18) | copy-start | bytes 49156
  6.5 58.1 %all-gather.2.cloned.1.call-start = ((), (), s32[]{:S(2)}) async-start(), calls=%async_computation.3 | async-start | bytes 5242880 | tf_op jit(solution)/shard_map/all_gather | solution.py:121
  9.0 14.6 %collective-permute-start = (bf16[3,9216]{1,0:T(4,128)(2,1)S(1)}, bf16[3,9216]{1,0:T(4,128)(2,1)S(1)}, u32[]{:S(2)}, u32[]{:S(2)}) collective-permute-start(bf16[3,9216]{1,0:T(4,128)(2,1)S(1)} %pad_maximum_fusion.2), channel_id=1, source_target_pairs={{0,1},{1,2},{2,3},{3,4},{4,5},{5,6},{6,7},{8,9},{9,10},{10,11},{11... | collective-permute-start | bytes 165896 | tf_op jit(solution)/shard_map/ppermute | solution.py:17
  15.8 14.4 %all-to-all-start = ((bf16[8,1,8]{2,1,0:T(2,128)(2,1)}), bf16[8,1,8]{2,1,0:T(2,128)(2,1)S(1)}, u32[]{:S(2)}, u32[]{:S(2)}) async-start(bf16[8,1,8]{2,1,0:T(2,128)(2,1)} %convert_element_type.119), calls=%async_computation | async-start | bytes 8192 | tf_op jit(solution)/shard_map/all_to_all | solution.py:128
  25.8 1.0 copy-start
  30.2 5.2 %copy-start.6 = (s32[4]{0:T(128)S(1)}, s32[4]{0:T(128)}, u32[]{:S(2)}) copy-start(s32[4]{0:T(128)} %param.22) | copy-start | bytes 52
  30.2 7.1 %copy-start.7 = (s32[4]{0:T(128)S(1)}, s32[4]{0:T(128)}, u32[]{:S(2)}) copy-start(s32[4]{0:T(128)} %param.21) | copy-start | bytes 52
  30.2 54.3 %all-to-all-start.1 = ((bf16[8,8,128,128]{3,2,1,0:T(8,128)(2,1)}), bf16[8,8,128,128]{3,2,1,0:T(8,128)(2,1)S(1)}, u32[]{:S(2)}, u32[]{:S(2)}) async-start(bf16[8,8,128,128]{3,2,1,0:T(8,128)(2,1)} %bitcast.28), calls=%async_computation.1 | async-start | bytes 4194304 | tf_op jit(solution)/shard_map/all_to_all | solution.py:135
  91.9 53.4 %all-to-all-start.2 = ((bf16[8,8,128,128]{3,2,1,0:T(8,128)(2,1)}), bf16[8,8,128,128]{3,2,1,0:T(8,128)(2,1)}, u32[]{:S(2)}, u32[]{:S(2)}) async-start(bf16[8,8,128,128]{3,2,1,0:T(8,128)(2,1)} %get-tuple-element.32), calls=%async_computation.2 | async-start | bytes 4194304 | tf_op jit(solution)/shard_map/all_to_all | solution.py:146
  147.8 2.6 %copy-start.1 = (bf16[8,8,64,128]{3,2,1,0:T(8,128)(2,1)S(1)}, bf16[8,8,64,128]{3,2,1,0:T(8,128)(2,1)}, u32[]{:S(2)}) copy-start(bf16[8,8,64,128]{3,2,1,0:T(8,128)(2,1)} %copy-done) | copy-start | bytes 3145732
  165.0 2.8 %copy-start.4 = (f32[8192]{0:T(1024)S(1)}, f32[8192]{0:T(1024)}, u32[]{:S(2)}) copy-start(f32[8192]{0:T(1024)} %param.19) | copy-start | bytes 98308
Sparse Core Ops, SparseCore 0:
  9.2 55.3 all-gather.1
where the time goes:
time: 180 us; the launch traced here: 179 us
  waiting for transfers between devices  90.8 us (50%)
  local copies, waits for them, and re-layouts  36 us (20%)
  starting transfers between devices  18.1 us (10%)
  between operations  16.2 us (9%)
  matrix products  9.01 us (5%)
  other arithmetic  8.74 us (5%)
    all_to_all x1, waiting for transfers between devices, body(): lax.all_to_all(incoming_parts.astype(jnp.bfloat16), 'ctx', split_axis=0,...  45.1 us
    all_gather x1, waiting for transfers between devices, body(): pooled = lax.all_gather(cache_pool, 'batch', axis=0, tiled=True)  26.1 us
    all_to_all x1, waiting for transfers between devices, body(): lax.all_to_all(end_state.reshape(ctx_count, head_share, P_SIZE, N), 'ctx'...  18.9 us
    all_to_all x1, starting transfers between devices, body(): lax.all_to_all(block_decay.reshape(ctx_count, head_share), 'ctx', split_a...  6.16 us
    dynamic_update_slice x8, local copies, waits for them, and re-layouts, body(): lax.scan(advance, start_state.astype(jnp.float32), (decays_in, states_in))  5.97 us
    all_to_all x1, starting transfers between devices, body(): lax.all_to_all(end_state.reshape(ctx_count, head_share, P_SIZE, N), 'ctx'...  5.24 us
    mul x2, local copies, waits for them, and re-layouts, block_output(): result = summed * inv_scale * norm_gain.reshape(LOCAL_HEADS, P_SIZE)  4.69 us
    all_to_all x1, starting transfers between devices, body(): lax.all_to_all(incoming_parts.astype(jnp.bfloat16), 'ctx', split_axis=0,...  4.35 us
  transfers between devices with their start and end apart: 5, of which 3 were waited for; matrix products, arithmetic and copies ran while one was open for 10% of the time, Pallas kernels for 0%

commit v1 on v0

--- a/solution.py
+++ b/solution.py
@@ -118,7 +118,23 @@
     cache_owner = reuse_owner[request]
     cached_level = reuse_level[request]
     slots = cache_pool.shape[0]
-    pooled = lax.all_gather(cache_pool, "batch", axis=0, tiled=True)
+    ways, here, step = (lax.axis_size("batch"), lax.axis_index("batch"), cache_pool.shape[0])
+    dims = [n * ways if d == 0 else n for d, n in enumerate(cache_pool.shape)]
+    full = lax.dynamic_update_slice_in_dim(
+        jnp.zeros(dims, cache_pool.dtype), cache_pool, here * step, axis=0
+    )
+    going_up = going_down = cache_pool
+    for far in range(1, ways // 2 + 1):
+        going_up = lax.ppermute(going_up, "batch", [(d, (d + 1) % ways) for d in range(ways)])
+        full = lax.dynamic_update_slice_in_dim(full, going_up, (here - far) % ways * step, axis=0)
+        if 2 * far < ways:
+            going_down = lax.ppermute(
+                going_down, "batch", [(d, (d - 1) % ways) for d in range(ways)]
+            )
+            full = lax.dynamic_update_slice_in_dim(
+                full, going_down, (here + far) % ways * step, axis=0
+            )
+    pooled = full
     slot_index = cache_owner * slots + jnp.maximum(cached_level - 1, 0)
     start_state = lax.dynamic_index_in_dim(pooled, slot_index, 0, keepdims=False)
     start_state = jnp.where(cached_level > 0, start_state, jnp.zeros_like(start_state))

time: 180 us -> 193 us (1.072)
  waiting for transfers between devices: 90.8 us -> 106 us
  between operations: 16.2 us -> 2.69 us
  local copies, waits for them, and re-layouts: 36 us -> 42.5 us
  starting transfers between devices: 18.1 us -> 22 us
    ppermute x0 -> x3, waiting for transfers between devices: none -> 61.1 us  [the longest x2 44.9 us: body(): lax.ppermute(going_up, 'batch', [(d, (d + 1) % ways) for d in range(ways)])]
    all_gather x1 -> x0, waiting for transfers between devices: 26.1 us -> none  [body(): pooled = lax.all_gather(cache_pool, 'batch', axis=0, tiled=True)]
    all_to_all x1, waiting for transfers between devices: 18.9 us -> 0.01 us  [body(): lax.all_to_all(end_state.reshape(ctx_count, head_share, P_SIZE, N), 'ctx'...]
    dynamic_update_slice x0 -> x4, local copies, waits for them, and re-layouts: none -> 4.34 us  [the longest x2 2.81 us: body(): lax.dynamic_update_slice_in_dim(full, going_up, (here - far) % ways * ste...]
    ppermute x0 -> x3, starting transfers between devices: none -> 3.52 us  [the longest x2 2.08 us: body(): lax.ppermute(going_up, 'batch', [(d, (d + 1) % ways) for d in range(ways)])]
  transfers between devices with their start and end apart: 5 -> 7, of which waited for: 3 -> 4; matrix products, arithmetic and copies ran while one was open for 10% -> 12% of each run, Pallas kernels for 0% -> 0%
where the time goes in v1:
time: 193 us; the launch traced here: 192 us
  waiting for transfers between devices  106 us (55%)
  local copies, waits for them, and re-layouts  42.5 us (22%)
  starting transfers between devices  22 us (11%)
  matrix products  8.99 us (5%)
  other arithmetic  8.95 us (5%)
  between operations  2.69 us (1%)
    all_to_all x1, waiting for transfers between devices, body(): lax.all_to_all(incoming_parts.astype(jnp.bfloat16), 'ctx', split_axis=0,...  45.2 us
    ppermute x2, waiting for transfers between devices, body(): lax.ppermute(going_up, 'batch', [(d, (d + 1) % ways) for d in range(ways)])  44.9 us
    ppermute x1, waiting for transfers between devices, body(): lax.ppermute(going_down, 'batch', [(d, (d - 1) % ways) for d in range(way...  16.2 us
    all_to_all x1, starting transfers between devices, body(): lax.all_to_all(block_decay.reshape(ctx_count, head_share), 'ctx', split_a...  6.16 us
    dynamic_update_slice x8, local copies, waits for them, and re-layouts, body(): lax.scan(advance, start_state.astype(jnp.float32), (decays_in, states_in))  5.97 us
    all_to_all x1, starting transfers between devices, body(): lax.all_to_all(end_state.reshape(ctx_count, head_share, P_SIZE, N), 'ctx'...  5.24 us
    all_to_all x1, starting transfers between devices, body(): lax.all_to_all(incoming_parts.astype(jnp.bfloat16), 'ctx', split_axis=0,...  4.75 us
    mul x2, local copies, waits for them, and re-layouts, block_output(): result = summed * inv_scale * norm_gain.reshape(LOCAL_HEADS, P_SIZE)  4.68 us
  transfers between devices with their start and end apart: 7, of which 4 were waited for; matrix products, arithmetic and copies ran while one was open for 12% of the time, Pallas kernels for 0%

profile of v1, /device:TPU:0, one launch (start us, length us, event | category | flops | bytes accessed | tf_op | source)
XLA Modules:
  0.0 191.6 jit_solution(3679133486284647897)
XLA Ops:
  1.8 2.4 %collective-permute-start = (bf16[3,9216]{1,0:T(4,128)(2,1)S(1)}, bf16[3,9216]{1,0:T(4,128)(2,1)S(1)}, u32[]{:S(2)}, u32[]{:S(2)}) collective-permute-start(bf16[3,9216]{1,0:T(4,128)(2,1)S(1)} %pad_maximum_fusion.2), channel_id=1, source_target_pairs={{0,1},{1,2},{2,3},{3,4},{4,5},{5,6},{6,7},{8,9},{9,10},{10,11},{11... | collective-permute-start | bytes 165896 | tf_op jit(solution)/shard_map/ppermute | solution.py:17
  8.6 6.2 %all-to-all-start = ((bf16[8,1,8]{2,1,0:T(2,128)(2,1)}), bf16[8,1,8]{2,1,0:T(2,128)(2,1)S(1)}, u32[]{:S(2)}, u32[]{:S(2)}) async-start(bf16[8,1,8]{2,1,0:T(2,128)(2,1)} %convert_element_type.119), calls=%async_computation | async-start | bytes 8192 | tf_op jit(solution)/shard_map/all_to_all | solution.py:144
  18.8 1.6 fusion.16
  21.7 3.4 %convolution_convert_fusion = bf16[4,16,128,128]{3,2,1,0:T(8,128)(2,1)} fusion(f32[64,4,16]{0,2,1:T(8,128)S(1)} %get-tuple-element.54, bf16[64,4,16,128]{3,2,1,0:T(8,128)(2,1)S(1)} %bitcast.84, bf16[64,4,128,1]{2,1,0,3:T(4,128)(2,1)S(1)} %bitcast.90), kind=kOutput, calls=%fused_computation.12 | convolution fusion | flops 136839168 | bytes 3227648 | tf_op jit(solution)/shard_map/sgkp,sgn->gkpn/dot_general | solution.py:54
  25.1 5.2 %all-to-all-start.1 = ((bf16[8,8,128,128]{3,2,1,0:T(8,128)(2,1)}), bf16[8,8,128,128]{3,2,1,0:T(8,128)(2,1)S(1)}, u32[]{:S(2)}, u32[]{:S(2)}) async-start(bf16[8,8,128,128]{3,2,1,0:T(8,128)(2,1)} %bitcast.28), calls=%async_computation.1 | async-start | bytes 4194304 | tf_op jit(solution)/shard_map/all_to_all | solution.py:151
  30.4 1.5 collective-permute-start.1
  31.8 1.4 collective-permute-start.2
  33.3 24.2 %collective-permute-done.1 = bf16[4,8,128,128]{3,2,1,0:T(8,128)(2,1)} collective-permute-done((bf16[4,8,128,128]{3,2,1,0:T(8,128)(2,1)}, bf16[4,8,128,128]{3,2,1,0:T(8,128)(2,1)}, u32[]{:S(2)}, u32[]{:S(2)}) %collective-permute-start.1) | collective-permute-done | bytes 1048608 | tf_op jit(solution)/shard_map/ppermute | solution.py:128
  63.9 16.2 %collective-permute-done.2 = bf16[4,8,128,128]{3,2,1,0:T(8,128)(2,1)} collective-permute-done((bf16[4,8,128,128]{3,2,1,0:T(8,128)(2,1)}, bf16[4,8,128,128]{3,2,1,0:T(8,128)(2,1)}, u32[]{:S(2)}, u32[]{:S(2)}) %collective-permute-start.2) | collective-permute-done | bytes 1048608 | tf_op jit(solution)/shard_map/ppermute | solution.py:131
  81.5 20.6 %collective-permute-done.3 = bf16[4,8,128,128]{3,2,1,0:T(8,128)(2,1)} collective-permute-done((bf16[4,8,128,128]{3,2,1,0:T(8,128)(2,1)}, bf16[4,8,128,128]{3,2,1,0:T(8,128)(2,1)}, u32[]{:S(2)}, u32[]{:S(2)}) %collective-permute-start.3) | collective-permute-done | bytes 1048608 | tf_op jit(solution)/shard_map/ppermute | solution.py:128
  103.6 7.4 %while.12 = (s32[]{:T(128)}, f32[8,128,128]{2,1,0:T(8,128)S(1)}, bf16[8,8,128,128]{3,2,1,0:T(8,128)(2,1)}, bf16[8,8]{1,0:T(8,128)(2,1)S(1)}, bf16[8,8,128,128]{3,2,1,0:T(8,128)(2,1)S(1)}, /*index=5*/s32[]{:T(128)}) while((s32[]{:T(128)}, f32[8,128,128]{2,1,0:T(8,128)S(1)}, bf16[8,8,128,128]{3,2,1,0:T(8,128)(2,1)}, bf16[8,8]{1,0:T(8,128)(2,1)S(1)}, ...), condition=%wide.region_2.3_spmd, body=%wide.region_1.2_spmd.sunk | while | flops 393226 | bytes 2359965 | solution.py:159
  111.0 4.8 %all-to-all-start.2 = ((bf16[8,8,128,128]{3,2,1,0:T(8,128)(2,1)}), bf16[8,8,128,128]{3,2,1,0:T(8,128)(2,1)}, u32[]{:S(2)}, u32[]{:S(2)}) async-start(bf16[8,8,128,128]{3,2,1,0:T(8,128)(2,1)} %get-tuple-element.32), calls=%async_computation.2 | async-start | bytes 4194304 | tf_op jit(solution)/shard_map/all_to_all | solution.py:162
  115.8 1.9 %mul.269 = f32[64,64,128]{2,1,0:T(8,128)} broadcast(f32[64,64]{1,0:T(8,128)S(1)} %exp.43), dimensions={0,1} | broadcast | bytes 2113536 | tf_op jit(solution)/shard_map/mul | solution.py:70
  117.8 1.7 mul.270
  119.7 45.2 %all-to-all-done.2 = bf16[8,8,128,128]{3,2,1,0:T(8,128)(2,1)} async-done(((bf16[8,8,128,128]{3,2,1,0:T(8,128)(2,1)}), bf16[8,8,128,128]{3,2,1,0:T(8,128)(2,1)}, u32[]{:S(2)}, u32[]{:S(2)}) %all-to-all-start.2) | async-done | bytes 2097184 | tf_op jit(solution)/shard_map/all_to_all | solution.py:162
  164.9 2.4 %fusion.4 = f32[64,4,16,128]{3,0,2,1:T(8,128)S(1)} fusion(bf16[64,4,128,1]{2,1,0,3:T(4,128)(2,1)S(1)} %bitcast.89, bf16[4,16,128,128]{3,2,1,0:T(8,128)(2,1)} %bitcast.77), kind=kOutput, calls=%fused_computation.13 | convolution fusion | flops 134217728 | bytes 4259840 | tf_op jit(solution)/shard_map/tgn,gkpn->tgkp/dot_general | solution.py:67
  167.4 2.5 %copy.59 = f32[64,4,16,128]{3,2,1,0:T(8,128)} copy(f32[64,4,16,128]{3,0,2,1:T(8,128)S(1)} %fusion.4) | data formatting | bytes 4194304 | tf_op jit(solution)/shard_map/tgn,gkpn->tgkp/transpose | solution.py:67
  169.9 3.0 %multiply_reduce_fusion = (f32[64,4,16]{0,2,1:T(8,128)S(1)}, f32[64,4,16,128]{3,0,2,1:T(8,128)}) fusion(f32[64,4,16,128]{3,0,2,1:T(8,128)S(1)} %fusion.4, f32[64,4,16]{0,2,1:T(8,128)S(1)} %get-tuple-element.53, bf16[64,4,16,128]{3,2,1,0:T(8,128)(2,1)S(1)} %bitcast.85, f32[4,16,64]{2,1,0:T(8,128)S(1)} %bitcast.98, f32[4,16,64]{2,1,0:T(8,128)S(1)} %bitcast.99, ...), kind=kOutput, calls=%fused_computation.8 | convolution fusion | flops 70512640 | bytes 5378048 | tf_op jit(solution)/shard_map/gkts,sgkp->tgkp/dot_general | solution.py:47
  173.0 2.0 %mul.286 = f32[64,64,128]{2,1,0:T(8,128)} broadcast(f32[64,64]{1,0:T(8,128)S(1)} %copy.60), dimensions={0,1} | broadcast | bytes 2113536 | tf_op jit(solution)/shard_map/mul | solution.py:72
  174.9 2.7 %mul.287 = f32[1,64,8192]{2,1,0:T(8,128)} reshape(f32[64,64,128]{2,1,0:T(8,128)} %mul.286) | data formatting | bytes 4194304 | tf_op jit(solution)/shard_map/mul | solution.py:72
  177.7 4.1 %copy.52 = f32[64,4,16,128]{3,2,1,0:T(8,128)} copy(f32[64,4,16,128]{3,0,2,1:T(8,128)} %get-tuple-element.60) | data formatting | bytes 4194304 | tf_op jit(solution)/shard_map/gkts,sgkp->tgkp/transpose | solution.py:47
  181.8 2.7 %reshape.233 = f32[1,64,8192]{2,1,0:T(8,128)} reshape(f32[64,4,16,128]{3,2,1,0:T(8,128)} %copy.52) | data formatting | bytes 4194304 | tf_op jit(solution)/shard_map/reshape | solution.py:59
  184.6 2.8 %reshape.234 = f32[1,64,8192]{2,1,0:T(8,128)} reshape(f32[64,4,16,128]{3,2,1,0:T(8,128)} %copy.59) | data formatting | bytes 4194304 | tf_op jit(solution)/shard_map/reshape | solution.py:69
  187.3 4.3 %select_convert_fusion = bf16[1,64,8192]{2,1,0:T(8,128)(2,1)} fusion(f32[1,64,8192]{2,1,0:T(8,128)} %mul.287, f32[1,64,8192]{2,1,0:T(8,128)} %reshape.233, f32[1,64,8192]{2,1,0:T(8,128)S(1)} %mul.270, f32[1,64,8192]{2,1,0:T(8,128)} %reshape.234, f32[8192]{0:T(1024)S(1)} %copy-done.4, pred[64]{0:T(512)(128)(4,1)S(1)} %add_compare_fusion), kind=kLoop, calls=%fused_computation.7 | loop fusion | flops 3145728 | bytes 9470016 | tf_op jit(solution)/shard_map/convert_element_type | solution.py:74
  (84 shorter events, 25.8 us)
Async XLA Ops:
  0.0 18.8 %copy-start.2 = (bf16[1,64,8192]{2,1,0:T(8,128)(2,1)S(1)}, bf16[1,64,8192]{2,1,0:T(8,128)(2,1)}, u32[]{:S(2)}) copy-start(bf16[1,64,8192]{2,1,0:T(8,128)(2,1)} %param.13) | copy-start | bytes 3145732
  1.8 15.6 %collective-permute-start = (bf16[3,9216]{1,0:T(4,128)(2,1)S(1)}, bf16[3,9216]{1,0:T(4,128)(2,1)S(1)}, u32[]{:S(2)}, u32[]{:S(2)}) collective-permute-start(bf16[3,9216]{1,0:T(4,128)(2,1)S(1)} %pad_maximum_fusion.2), channel_id=1, source_target_pairs={{0,1},{1,2},{2,3},{3,4},{4,5},{5,6},{6,7},{8,9},{9,10},{10,11},{11... | collective-permute-start | bytes 165896 | tf_op jit(solution)/shard_map/ppermute | solution.py:17
  8.6 16.5 %all-to-all-start = ((bf16[8,1,8]{2,1,0:T(2,128)(2,1)}), bf16[8,1,8]{2,1,0:T(2,128)(2,1)S(1)}, u32[]{:S(2)}, u32[]{:S(2)}) async-start(bf16[8,1,8]{2,1,0:T(2,128)(2,1)} %convert_element_type.119), calls=%async_computation | async-start | bytes 8192 | tf_op jit(solution)/shard_map/all_to_all | solution.py:144
  20.7 1.0 copy-start
  25.1 33.0 %copy-start.5 = (s32[4]{0:T(128)S(1)}, s32[4]{0:T(128)}, u32[]{:S(2)}) copy-start(s32[4]{0:T(128)} %param.22) | copy-start | bytes 52
  25.1 33.6 %copy-start.6 = (s32[4]{0:T(128)S(1)}, s32[4]{0:T(128)}, u32[]{:S(2)}) copy-start(s32[4]{0:T(128)} %param.21) | copy-start | bytes 52
  25.1 78.4 %all-to-all-start.1 = ((bf16[8,8,128,128]{3,2,1,0:T(8,128)(2,1)}), bf16[8,8,128,128]{3,2,1,0:T(8,128)(2,1)S(1)}, u32[]{:S(2)}, u32[]{:S(2)}) async-start(bf16[8,8,128,128]{3,2,1,0:T(8,128)(2,1)} %bitcast.28), calls=%async_computation.1 | async-start | bytes 4194304 | tf_op jit(solution)/shard_map/all_to_all | solution.py:151
  30.4 27.2 %collective-permute-start.1 = (bf16[4,8,128,128]{3,2,1,0:T(8,128)(2,1)}, bf16[4,8,128,128]{3,2,1,0:T(8,128)(2,1)}, u32[]{:S(2)}, u32[]{:S(2)}) collective-permute-start(bf16[4,8,128,128]{3,2,1,0:T(8,128)(2,1)} %param.20), channel_id=1, source_target_pairs={{0,8},{8,16},{16,24},{24,0},{1,9},{9,17},{17,25},{25,1},{2,10},{10... | collective-permute-start | bytes 3145736 | tf_op jit(solution)/shard_map/ppermute | solution.py:128
  31.8 48.2 %collective-permute-start.2 = (bf16[4,8,128,128]{3,2,1,0:T(8,128)(2,1)}, bf16[4,8,128,128]{3,2,1,0:T(8,128)(2,1)}, u32[]{:S(2)}, u32[]{:S(2)}) collective-permute-start(bf16[4,8,128,128]{3,2,1,0:T(8,128)(2,1)} %param.20), channel_id=1, source_target_pairs={{0,24},{8,0},{16,8},{24,16},{1,25},{9,1},{17,9},{25,17},{2,26},{10... | collective-permute-start | bytes 3145736 | tf_op jit(solution)/shard_map/ppermute | solution.py:131
  57.5 44.6 %collective-permute-start.3 = (bf16[4,8,128,128]{3,2,1,0:T(8,128)(2,1)}, bf16[4,8,128,128]{3,2,1,0:T(8,128)(2,1)}, u32[]{:S(2)}, u32[]{:S(2)}) collective-permute-start(bf16[4,8,128,128]{3,2,1,0:T(8,128)(2,1)} %collective-permute-done.1), channel_id=1, source_target_pairs={{0,8},{8,16},{16,24},{24,0},{1,9},{9,17},{17,25},{25,1},{2,10},{10... | collective-permute-start | bytes 3145736 | tf_op jit(solution)/shard_map/ppermute | solution.py:128
  61.1 1.2 copy-start.3
  111.0 53.9 %all-to-all-start.2 = ((bf16[8,8,128,128]{3,2,1,0:T(8,128)(2,1)}), bf16[8,8,128,128]{3,2,1,0:T(8,128)(2,1)}, u32[]{:S(2)}, u32[]{:S(2)}) async-start(bf16[8,8,128,128]{3,2,1,0:T(8,128)(2,1)} %get-tuple-element.32), calls=%async_computation.2 | async-start | bytes 4194304 | tf_op jit(solution)/shard_map/all_to_all | solution.py:162
  167.3 2.6 %copy-start.1 = (bf16[8,8,64,128]{3,2,1,0:T(8,128)(2,1)S(1)}, bf16[8,8,64,128]{3,2,1,0:T(8,128)(2,1)}, u32[]{:S(2)}) copy-start(bf16[8,8,64,128]{3,2,1,0:T(8,128)(2,1)} %copy-done) | copy-start | bytes 3145732
  184.6 2.8 %copy-start.4 = (f32[8192]{0:T(1024)S(1)}, f32[8192]{0:T(1024)}, u32[]{:S(2)}) copy-start(f32[8192]{0:T(1024)} %param.19) | copy-start | bytes 98308
